TPU v7x, 512 devices: a whole 4x4x16 slice. The times are simulated.
512 devices in a mesh: blk: 128 (over y_lo, z, x), feat: 4 (over y_hi, core).
Axes of the slice: x: 4, y: 4 (y_hi: 2, y_lo: 2; y = y_hi * 2 + y_lo), z: 16, core: 2. Of those that a mesh axis runs over, the one named last changes fastest.
Arguments:
- image_embeds: bfloat16 [8192, 1024], P('blk', 'feat')
- text_embeds: bfloat16 [8192, 1024], P('blk', 'feat')
- logit_scale: float32 [1], replicated, may hold values from 3 to 6
Outputs:
- pair_loss: float32 [8192], P('blk')
- image_grad: float32 [8192, 1024], P('blk', 'feat')
- text_grad: float32 [8192, 1024], P('blk', 'feat')
All inputs are finite; a program needn't handle non-finite values.
Results may differ from a plain program's by a relative error of at most 0.004.
Values may be sent and summed in bfloat16 or wider, within the bound.
A program may use at most 64 MiB of HBM per device.

v0:
```python
import jax
import jax.numpy as jnp
from jax import lax
from jax.sharding import PartitionSpec as P


def column_lse(logits):
    local_max = jnp.max(logits, axis=0)
    largest = lax.pmax(local_max.astype(jnp.bfloat16), "blk").astype(local_max.dtype)
    summed = lax.psum(jnp.sum(jnp.exp(logits - largest[None, :]), axis=0), "blk")
    return largest + jnp.log(summed)


def per_device(image_embeds, text_embeds, logit_scale):
    factor = logit_scale[0]
    row_count = image_embeds.shape[0]
    position = lax.axis_index("blk")
    all_texts = lax.all_gather(text_embeds, "blk", axis=0, tiled=True)
    pair_count = all_texts.shape[0]
    partial_value = lax.dot_general(
        image_embeds, all_texts, (((1,), (1,)), ((), ())), preferred_element_type=jnp.float32
    )
    first_row = position * row_count
    row_ids = first_row + lax.iota(jnp.int32, row_count)
    unit_matrix = jnp.eye(row_count, dtype=jnp.float32)
    logits = factor * lax.psum(partial_value, "feat")
    row_max = jnp.max(logits, axis=1)
    row_lse = row_max + jnp.log(jnp.sum(jnp.exp(logits - row_max[:, None]), axis=1))
    col_lse = column_lse(logits)
    identity = (lax.iota(jnp.int32, pair_count)[None, :] == row_ids[:, None]).astype(jnp.float32)
    grad_logits = (
        0.5 * (jnp.exp(logits - row_lse[:, None]) + jnp.exp(logits - col_lse[None, :])) - identity
    ).astype(jnp.bfloat16)
    own_block = lax.dynamic_slice_in_dim(logits, first_row, row_count, 1)
    own_column = lax.dynamic_slice_in_dim(col_lse, first_row, row_count, 0)
    diagonal = jnp.sum(own_block * unit_matrix, axis=1)
    pair_loss = 0.5 * (row_lse + own_column) - diagonal
    image_grad = factor * jnp.dot(grad_logits, all_texts, preferred_element_type=jnp.float32)
    columns = lax.all_to_all(grad_logits, "blk", split_axis=1, concat_axis=0, tiled=True)
    text_acc = lax.dot_general(
        columns,
        lax.all_gather(image_embeds, "blk", axis=0, tiled=True),
        (((0,), (0,)), ((), ())),
        preferred_element_type=jnp.float32,
    )
    return (pair_loss, image_grad, factor * text_acc)


def solution(mesh):
    return jax.shard_map(
        per_device,
        mesh=mesh,
        in_specs=(P("blk", "feat"), P("blk", "feat"), P()),
        out_specs=(P("blk"), P("blk", "feat"), P("blk", "feat")),
        check_vma=False,
    )
```

profile of v0, /device:TPU:8, one launch (start us, length us, event | category | flops | bytes accessed | tf_op | source)
XLA Modules:
  0.0 1965.5 jit_solution(5668434748001290267)
XLA Ops:
  7.2 0.0 all-gather.3.cloned.1.call-start
  7.2 0.7 all-gather.3.cloned.1.call-update
  7.9 0.0 all-reduce.2.cloned.1.call-start
  7.9 600.5 %all-gather.3.cloned.1.call-done = bf16[8192,256]{1,0:T(8,128)(2,1)} async-done(((bf16[64,256]{1,0:T(8,128)(2,1)}), bf16[8192,256]{1,0:T(8,128)(2,1)}) %all-gather.3.cloned.1.call-update) | async-done | bytes 4194320 | tf_op jit(solution)/shard_map/all_gather | solution.py:18
  608.4 4.9 fusion.1
  613.3 0.0 all-reduce.2.cloned.1.call-update
  613.3 0.0 all-gather.5.cloned.1.call-start
  613.4 0.7 all-gather.5.cloned.1.call-update
  614.7 63.9 %all-reduce.2.cloned.1.call-done = f32[64,8192]{1,0:T(8,128)} async-done(((f32[64,8192]{1,0:T(8,128)}), f32[64,8192]{1,0:T(8,128)}) %all-reduce.2.cloned.1.call-update) | async-done | bytes 2097168 | tf_op jit(solution)/shard_map/psum | solution.py:26
  678.7 2.0 fusion
  680.7 611.8 %pmax.7 = bf16[8192]{0:T(1024)(128)(2,1)S(1)} all-reduce(bf16[8192]{0:T(1024)(128)(2,1)S(1)} %get-tuple-element.5), channel_id=1, replica_groups=mesh['blk'=128,'feat'=4] {'blk'}, use_global_device_ids=true, to_apply=%region_4.0 | all-reduce | flops 8192 | bytes 32768 | tf_op jit(solution)/shard_map/pmax | solution.py:9
  1292.5 0.2 select_reduce_fusion
  1292.6 0.8 exponential_reduce_fusion
  1293.4 606.4 %psum.15 = f32[8192]{0:T(1024)S(1)} all-reduce(f32[8192]{0:T(1024)S(1)} %get-tuple-element.3), channel_id=1, replica_groups=mesh['blk'=128,'feat'=4] {'blk'}, use_global_device_ids=true, to_apply=%region_6.0 | all-reduce | flops 8192 | bytes 65536 | tf_op jit(solution)/shard_map/psum | solution.py:10
  1899.8 0.6 multiply_subtract_fusion
  1900.4 0.8 subtract_convert_fusion
  1901.3 3.3 all_to_all.14
  1904.5 2.9 copy.11
  1907.5 2.3 reshape.22
  1909.8 7.1 all-to-all-start
  1916.9 3.6 convolution_multiply_fusion
  1920.5 31.1 %all-to-all-done = bf16[128,2,2048]{2,1,0:T(2,128)(2,1)} async-done(((bf16[128,2,2048]{2,1,0:T(2,128)(2,1)}), bf16[128,2,2048]{2,1,0:T(2,128)(2,1)}, u32[]{:S(2)}, u32[]{:S(2)}) %all-to-all-start) | async-done | bytes 1048608 | tf_op jit(solution)/shard_map/all_to_all | solution.py:39
  1951.6 3.8 reshape.23
  1955.4 0.0 all-gather.5.cloned.1.call-done
  1955.4 3.5 convolution_multiply_fusion.1
  (3 shorter events, 0.0 us)
Async XLA Ops:
  7.2 601.3 %all-gather.3.cloned.1.call-start = ((), (), s32[]{:S(2)}) async-start(), calls=%async_computation.1 | async-start | bytes 4227072 | tf_op jit(solution)/shard_map/all_gather | solution.py:18
  7.9 670.8 %all-reduce.2.cloned.1.call-start = ((), (), s32[]{:S(2)}) async-start(), calls=%async_computation.2 | async-start | bytes 4194304 | tf_op jit(solution)/shard_map/psum | solution.py:26
  613.3 1342.1 %all-gather.5.cloned.1.call-start = ((), (), s32[]{:S(2)}) async-start(), calls=%async_computation.3 | async-start | bytes 4227072 | tf_op jit(solution)/shard_map/all_gather | solution.py:42
  1909.8 41.9 %all-to-all-start = ((bf16[128,2,2048]{2,1,0:T(2,128)(2,1)}), bf16[128,2,2048]{2,1,0:T(2,128)(2,1)}, u32[]{:S(2)}, u32[]{:S(2)}) async-start(bf16[128,2,2048]{2,1,0:T(2,128)(2,1)} %reshape.22), calls=%async_computation | async-start | bytes 2097152 | tf_op jit(solution)/shard_map/all_to_all | solution.py:39
Sparse Core Ops, SparseCore 0:
  10.1 598.3 all-gather.2
  613.5 65.1 all-reduce.1
  681.0 594.5 all-gather.4
where the time goes:
time: 1970 us
  blocking collectives  1220 us (62%)
  waiting for transfers between devices  697 us (35%)
    pmax x1, blocking collectives, column_lse(): lax.pmax(local_max.astype(jnp.bfloat16), 'blk').astype(local_max.dtype)  612 us
    psum x1, blocking collectives, column_lse(): lax.psum(jnp.sum(jnp.exp(logits - largest[None, :]), axis=0), 'blk')  606 us
    all_gather x1, waiting for transfers between devices, per_device(): all_texts = lax.all_gather(text_embeds, 'blk', axis=0, tiled=True)  600 us
    psum x1, waiting for transfers between devices, per_device(): logits = factor * lax.psum(partial_value, 'feat')  63.9 us
  transfers between devices with their start and end apart: 4, of which 3 were waited for; matrix products, arithmetic and copies ran while one was open for 1% of the time, Pallas kernels for 0%

commit v1 on v0

v1 whole, which is shorter than its diff:
```python
import functools

import jax
import jax.numpy as jnp
from jax import lax
from jax.experimental import pallas as pl
from jax.experimental.pallas import tpu as pltpu
from jax.sharding import PartitionSpec as P

MESH = pl.DeviceIdType.MESH
F32 = jnp.float32
BF16 = jnp.bfloat16

NX, NY, NZ = 4, 4, 16
ROWS, FEATS = 64, 256
HALF = ROWS // 2
IMG = 16 * ROWS
TXT = 8 * HALF
LANES = 128

PLANE = [(dx, dy) for dx in range(NX) for dy in range(NY) if dx or dy]
COLUMN = [(dh, dk) for dk in (4, 3, 5, 2, 6, 1, 7, 0) for dh in range(2) if dh or dk]


def where_am_i():
    blk, feat = lax.axis_index("blk"), lax.axis_index("feat")
    x = blk % NX
    z = (blk // NX) % NZ
    yl = blk // (NX * NZ)
    yh = feat // 2
    return x, yl, yh, z, feat % 2


def device(x, yl, yh, z, c):
    return {"blk": (yl * NZ + z) * NX + x, "feat": yh * 2 + c}


def kernel(
    scale_ref, img_ref, txt_ref, loss_ref, ig_ref, tg_ref,
    img_all, txt_all, logits, e_row, e_col, grad, i_part, t_part, i_recv, t_recv,
    row_own, row_max, row_recv, row_lse, row_mul, col_own, col_recv, loss_all, pair_out, pair_in,
    s_txt, r_txt, s_img, r_img, s_pair, r_pair, s_sib, r_sib,
    s_row, r_row, s_col, r_col, s_loss, r_loss, s_tp, r_tp, s_ip, r_ip, s_fin, r_fin,
):
    x, yl, yh, z, c = where_am_i()
    q, k = z % 2, z // 2
    feat = yh * 2 + c
    factor = scale_ref[0]

    def in_plane(dx, dy, dq=0):
        x2 = (x + dx) % NX
        y2 = (yh * 2 + yl + dy) % NY
        return x2, y2 % 2, y2 // 2, (z + dq) - 2 * dq * q

    def in_column(dh, dk):
        return x, yl, (yh + dh) % 2, ((k + dk) % 8) * 2 + q

    def to(place):
        return device(*place, c)

    pair = to((x, yl, yh, z + 1 - 2 * q))
    sibling = device(x, yl, yh, z, 1 - c)

    barrier = pltpu.get_barrier_semaphore()
    partners = [to(in_column(dh, dk)) for dh, dk in COLUMN]
    partners += [pair]
    partners += [to(in_plane(dx, dy, dq)) for dq in range(2) for dx, dy in PLANE if dq or (dx, dy) != (0, 2)]
    partners += [sibling]
    for partner in partners:
        pl.semaphore_signal(barrier, inc=1, device_id=partner, device_id_type=MESH)

    def image_rows(q0, p0):
        return pl.ds(pl.multiple_of((q0 * 8 + p0) * ROWS, ROWS), ROWS)

    p = yl * NX + x
    own_rows = image_rows(q, p)
    own_cols = pl.ds(pl.multiple_of(k * HALF, HALF), HALF)
    own_half = pl.ds(pl.multiple_of(yh * HALF, HALF), HALF)
    img_all[feat, own_rows, :] = img_ref[...]
    txt_all[feat, own_cols, :] = txt_ref[own_half, :]
    col_own[...] = jnp.zeros_like(col_own)
    pl.semaphore_wait(barrier, len(partners))

    started = []

    def send(src, dst, s, r, target):
        copy = pltpu.make_async_remote_copy(
            src_ref=src, dst_ref=dst, send_sem=s, recv_sem=r, device_id=target, device_id_type=MESH
        )
        copy.start()
        started.append(copy)
        return copy

    txt_copies = []
    for n, (dh, dk) in enumerate(COLUMN):
        place = in_column(dh, dk)
        half = pl.ds(pl.multiple_of(place[2] * HALF, HALF), HALF)
        txt_copies.append(
            send(txt_ref.at[half, :], txt_all.at[feat, own_cols, :], s_txt.at[n], r_txt.at[n], to(place))
        )
    own_block = img_all.at[feat, own_rows, :]
    swap = send(img_ref, own_block, s_pair, r_pair, pair)
    direct = [
        send(img_ref, own_block, s_img.at[0, n], r_img.at[0, n], to(in_plane(dx, dy)))
        for n, (dx, dy) in enumerate(PLANE)
    ]
    swap.wait_recv()
    pair_block = img_all.at[feat, image_rows(1 - q, p), :]
    passed = [
        send(pair_block, pair_block, s_img.at[1, n], r_img.at[1, n], to(in_plane(dx, dy)))
        for n, (dx, dy) in enumerate(PLANE)
    ]

    def share_image(slot, q0):
        copies = []
        for h in range(2):
            part = img_all.at[2 * h + c, pl.ds(pl.multiple_of(q0 * 8 * ROWS, 8 * ROWS), 8 * ROWS), :]
            copies.append(send(part, part, s_sib.at[slot, h], r_sib.at[slot, h], sibling))
        return copies

    shared = []
    for copy in direct:
        copy.wait_recv()
    shared += share_image(0, q)
    for copy in txt_copies:
        copy.wait_recv()
    for h in range(2):
        part = txt_all.at[2 * h + c]
        shared.append(send(part, part, s_sib.at[1, h], r_sib.at[1, h], sibling))
    for copy in passed:
        copy.wait_recv()
    shared += share_image(2, 1 - q)
    for copy in shared:
        copy.wait_recv()

    eye = lax.broadcasted_iota(jnp.int32, (LANES, LANES), 0) == lax.broadcasted_iota(jnp.int32, (LANES, LANES), 1)

    def to_lanes(column):
        return jnp.sum(jnp.where(eye, column, 0.0), axis=0, keepdims=True)

    def to_rows(lanes):
        return jnp.sum(jnp.where(eye, lanes, 0.0), axis=1, keepdims=True)

    col_max = None
    for b in range(IMG // LANES):
        rows = pl.ds(b * LANES, LANES)
        total = None
        for f in range(4):
            term = lax.dot_general(
                img_all[f, rows, :], txt_all[f], (((1,), (1,)), ((), ())), preferred_element_type=F32
            )
            total = term if total is None else total + term
        value = factor * total
        logits[rows, :] = value
        largest = jnp.max(value, axis=1, keepdims=True)
        shifted = jnp.exp(value - largest)
        e_row[rows, :] = shifted
        lse = largest + jnp.log(jnp.sum(shifted, axis=1, keepdims=True))
        row_own[pl.ds(b, 1), :] = to_lanes(lse)
        row_max[pl.ds(b, 1), :] = to_lanes(largest)
        block_max = jnp.max(value, axis=0, keepdims=True)
        col_max = block_max if col_max is None else jnp.maximum(col_max, block_max)

    row_slot = row_recv.at[q * 16 + (yh * 2 + yl) * NX + x]
    row_copies = []
    for dq in range(2):
        for n, (dx, dy) in enumerate([(0, 0)] + PLANE):
            if dq or n:
                row_copies.append(
                    send(row_own, row_slot, s_row.at[dq, n], r_row.at[dq, n], to(in_plane(dx, dy, dq)))
                )
    row_slot[...] = row_own[...]

    col_sum = jnp.zeros((1, TXT), F32)
    for b in range(IMG // LANES):
        rows = pl.ds(b * LANES, LANES)
        shifted = jnp.exp(logits[rows, :] - col_max)
        e_col[rows, :] = shifted
        col_sum = col_sum + jnp.sum(shifted, axis=0, keepdims=True)
    lse = col_max + jnp.log(col_sum)
    col_own[pl.ds(0, 1), :] = lse[:, :LANES]
    col_own[pl.ds(1, 1), :] = lse[:, LANES:]
    col_slot = col_recv.at[k]
    col_copies = [
        send(col_own, col_slot, s_col.at[dk], r_col.at[dk], to(in_column(0, dk))) for dk in (4, 3, 5, 2, 6, 1, 7)
    ]
    col_slot[...] = col_own[...]

    for copy in row_copies:
        copy.wait_recv()
    for copy in col_copies:
        copy.wait_recv()

    def combine(parts):
        largest = jnp.max(parts, axis=0)
        return largest + jnp.log(jnp.sum(jnp.exp(parts - largest[None]), axis=0))

    row_total = combine(row_recv[...])
    row_lse[...] = row_total
    row_mul[...] = 0.5 * jnp.exp(row_max[...] - row_total)
    col_total = combine(col_recv[...])
    col_lse = jnp.concatenate([col_total[0:1], col_total[1:2]], axis=1)
    col_mul = 0.5 * jnp.exp(col_max - col_lse)

    for b in range(IMG // LANES):
        rows = pl.ds(b * LANES, LANES)
        row_factor = to_rows(row_mul[pl.ds(b, 1), :])
        grad[rows, :] = (e_row[rows, :] * row_factor + e_col[rows, :] * col_mul).astype(BF16)
    first = (q * 8 + p) * ROWS + yh * HALF
    diag_rows = pl.ds(pl.multiple_of(first, HALF), HALF)
    row_id = lax.broadcasted_iota(jnp.int32, (HALF, LANES), 0)
    lane_id = lax.broadcasted_iota(jnp.int32, (HALF, LANES), 1)
    pick = lane_id - first % LANES == row_id
    line = pl.ds(first // LANES, 1)
    diag_mul = jnp.sum(jnp.where(pick, row_mul[line, :], 0.0), axis=1, keepdims=True)
    diag_lse = jnp.sum(jnp.where(pick, row_lse[line, :], 0.0), axis=1, keepdims=True)
    row_id = lax.broadcasted_iota(jnp.int32, (HALF, TXT), 0)
    lane_id = lax.broadcasted_iota(jnp.int32, (HALF, TXT), 1)
    unit = lane_id - k * HALF == row_id
    grad[diag_rows, :] = (
        e_row[diag_rows, :] * diag_mul + e_col[diag_rows, :] * col_mul - unit.astype(F32)
    ).astype(BF16)
    loss = jnp.sum(
        jnp.where(unit, 0.5 * (diag_lse + col_lse) - logits[diag_rows, :], 0.0), axis=1, keepdims=True
    )
    loss_all[own_half, :] = jnp.broadcast_to(loss, (HALF, LANES))
    loss_part = loss_all.at[own_half, :]
    loss_copy = send(loss_part, loss_part, s_loss, r_loss, to(in_column(1, 0)))

    for h in range(2):
        t_part[h] = lax.dot_general(
            grad[...], img_all[2 * h + c], (((0,), (0,)), ((), ())), preferred_element_type=F32
        ).astype(BF16)
    tp_copies = []
    for n, (dh, dk) in enumerate(COLUMN):
        place = in_column(dh, dk)
        rows = pl.ds(pl.multiple_of(((k + dk) % 8) * HALF, HALF), HALF)
        tp_copies.append(
            send(t_part.at[place[2], rows, :], t_recv.at[yh, k], s_tp.at[n], r_tp.at[n], to(place))
        )
    t_recv[yh, k] = t_part[yh, own_cols, :]

    ip_copies = []
    for turn in range(2):
        q2 = 1 - q if turn == 0 else q
        rows = pl.ds(pl.multiple_of(q2 * 8 * ROWS, 8 * ROWS), 8 * ROWS)
        for h in range(2):
            i_part[h, rows, :] = jnp.dot(
                grad[rows, :], txt_all[2 * h + c], preferred_element_type=F32
            ).astype(BF16)
        slot = (yh * 2 + yl) * NX + x
        copies = []
        for n, (dx, dy) in enumerate(PLANE):
            place = in_plane(dx, dy)
            block = i_part.at[place[2], image_rows(q2, place[1] * NX + place[0]), :]
            copies.append(send(block, i_recv.at[turn, slot], s_ip.at[turn, n], r_ip.at[turn, n], to(place)))
        i_recv[turn, slot] = i_part[yh, image_rows(q2, p), :]
        ip_copies.append(copies)

    def total_of(ref, count):
        value = ref[0].astype(F32)
        for n in range(1, count):
            value = value + ref[n].astype(F32)
        return value

    for copy in ip_copies[0]:
        copy.wait_recv()
    pair_out[...] = total_of(i_recv.at[0], 16)
    final = send(pair_out, pair_in, s_fin, r_fin, pair)
    for copy in tp_copies:
        copy.wait_recv()
    for h in range(2):
        tg_ref[pl.ds(h * HALF, HALF), :] = total_of(t_recv.at[h], 8)
    loss_copy.wait_recv()
    square = lax.broadcasted_iota(jnp.int32, (ROWS, LANES), 0) == lax.broadcasted_iota(jnp.int32, (ROWS, LANES), 1)
    loss_ref[...] = jnp.sum(jnp.where(square, loss_all[...], 0.0), axis=0, keepdims=True)[:, :ROWS]
    for copy in ip_copies[1]:
        copy.wait_recv()
    own = total_of(i_recv.at[1], 16)
    final.wait_recv()
    ig_ref[...] = own + pair_in[...]
    for copy in started:
        copy.wait_send()


def per_device(image_embeds, text_embeds, logit_scale):
    vmem = pl.BlockSpec(memory_space=pltpu.VMEM)
    dma = pltpu.SemaphoreType.DMA
    column, plane = len(COLUMN), len(PLANE)
    loss, image_grad, text_grad = pl.pallas_call(
        kernel,
        out_shape=(
            jax.ShapeDtypeStruct((1, ROWS), F32),
            jax.ShapeDtypeStruct((ROWS, FEATS), F32),
            jax.ShapeDtypeStruct((ROWS, FEATS), F32),
        ),
        in_specs=[pl.BlockSpec(memory_space=pltpu.SMEM), vmem, vmem],
        out_specs=(vmem, vmem, vmem),
        scratch_shapes=[
            pltpu.VMEM((4, IMG, FEATS), BF16),
            pltpu.VMEM((4, TXT, FEATS), BF16),
            pltpu.VMEM((IMG, TXT), F32),
            pltpu.VMEM((IMG, TXT), F32),
            pltpu.VMEM((IMG, TXT), F32),
            pltpu.VMEM((IMG, TXT), BF16),
            pltpu.VMEM((2, IMG, FEATS), BF16),
            pltpu.VMEM((2, TXT, FEATS), BF16),
            pltpu.VMEM((2, 16, ROWS, FEATS), BF16),
            pltpu.VMEM((2, 8, HALF, FEATS), BF16),
            pltpu.VMEM((8, LANES), F32),
            pltpu.VMEM((8, LANES), F32),
            pltpu.VMEM((32, 8, LANES), F32),
            pltpu.VMEM((8, LANES), F32),
            pltpu.VMEM((8, LANES), F32),
            pltpu.VMEM((8, LANES), F32),
            pltpu.VMEM((8, 8, LANES), F32),
            pltpu.VMEM((ROWS, LANES), F32),
            pltpu.VMEM((ROWS, FEATS), F32),
            pltpu.VMEM((ROWS, FEATS), F32),
            dma((column,)), dma((column,)),
            dma((2, plane)), dma((2, plane)),
            dma, dma,
            dma((3, 2)), dma((3, 2)),
            dma((2, 16)), dma((2, 16)),
            dma((8,)), dma((8,)),
            dma, dma,
            dma((column,)), dma((column,)),
            dma((2, plane)), dma((2, plane)),
            dma, dma,
        ],
        compiler_params=pltpu.CompilerParams(
            collective_id=0, has_side_effects=True, vmem_limit_bytes=48 << 20
        ),
    )(logit_scale, image_embeds, text_embeds)
    factor = logit_scale[0]
    return loss.reshape(ROWS), factor * image_grad, factor * text_grad


def solution(mesh):
    return jax.shard_map(
        per_device,
        mesh=mesh,
        in_specs=(P("blk", "feat"), P("blk", "feat"), P()),
        out_specs=(P("blk"), P("blk", "feat"), P("blk", "feat")),
        check_vma=False,
    )
```

time: 1970 us -> 75.7 us (0.04)
  the two profiles are of different devices: /device:TPU:8 before, /device:TPU:1 now
where the time goes in v1:
time: 75.7 us; the launch traced here: 74.9 us
  Pallas kernels  71 us (94%)
  local copies, waits for them, and re-layouts  2.02 us (3%)
  between operations  1.3 us (2%)
    pallas_call x1, Pallas kernels, per_device(): pl.pallas_call(kernel, out_shape=(jax.ShapeDtypeStruct((1, ROWS), F32), j...  71 us
    unnamed x5, local copies, waits for them, and re-layouts  2.02 us

profile of v1, /device:TPU:1, one launch (start us, length us, event | category | flops | bytes accessed | tf_op | source)
XLA Modules:
  0.0 74.9 jit_solution(5188938762606472076)
XLA Ops:
  1.3 0.0 copy-start
  1.3 0.7 copy-done
  2.0 0.0 copy-start.1
  2.0 0.8 %copy-done.1 = bf16[64,256]{1,0:T(8,128)(2,1)S(1)} copy-done((bf16[64,256]{1,0:T(8,128)(2,1)S(1)}, bf16[64,256]{1,0:T(8,128)(2,1)}, u32[]{:S(2)}) %copy-start.1) | copy-done | bytes 32792
  2.8 71.0 %shard_map.58 = (f32[1,64]{1,0:T(1,128)S(1)}, f32[64,256]{1,0:T(8,128)S(1)}, f32[64,256]{1,0:T(8,128)S(1)}) custom-call(f32[1]{0:T(128)} %copy.7.scale_ref, bf16[64,256]{1,0:T(8,128)(2,1)S(1)} %copy-done, bf16[64,256]{1,0:T(8,128)(2,1)S(1)} %copy-done.1), custom_call_target="tpu_custom_call" | custom-call | tf_op jit(solution)/shard_map/pallas_call | solution.py:290
  73.8 0.7 broadcast_multiply_fusion
  74.4 0.5 copy.8
Async XLA Ops:
  1.3 0.8 %copy-start = (bf16[64,256]{1,0:T(8,128)(2,1)S(1)}, bf16[64,256]{1,0:T(8,128)(2,1)}, u32[]{:S(2)}) copy-start(bf16[64,256]{1,0:T(8,128)(2,1)} %img_ref.1) | copy-start | bytes 98308
  2.0 0.8 %copy-start.1 = (bf16[64,256]{1,0:T(8,128)(2,1)S(1)}, bf16[64,256]{1,0:T(8,128)(2,1)}, u32[]{:S(2)}) copy-start(bf16[64,256]{1,0:T(8,128)(2,1)} %txt_ref.1) | copy-start | bytes 98308

commit v2 on v1

--- a/solution.py
+++ b/solution.py
@@ -19,7 +19,8 @@
 LANES = 128
 
 PLANE = [(dx, dy) for dx in range(NX) for dy in range(NY) if dx or dy]
-COLUMN = [(dh, dk) for dk in (4, 3, 5, 2, 6, 1, 7, 0) for dh in range(2) if dh or dk]
+FAR = (4, 3, 5, 2, 6, 1, 7)
+COLUMN = [(dh, dk) for dk in FAR for dh in range(2)] + [(1, 0)]
 
 
 def where_am_i():
@@ -36,11 +37,12 @@
 
 
 def kernel(
-    scale_ref, img_ref, txt_ref, loss_ref, ig_ref, tg_ref,
+    scale_ref, img_hbm, txt_hbm, loss_ref, ig_ref, tg_ref,
+    txt_own,
     img_all, txt_all, logits, e_row, e_col, grad, i_part, t_part, i_recv, t_recv,
     row_own, row_max, row_recv, row_lse, row_mul, col_own, col_recv, loss_all, pair_out, pair_in,
-    s_txt, r_txt, s_img, r_img, s_pair, r_pair, s_sib, r_sib,
-    s_row, r_row, s_col, r_col, s_loss, r_loss, s_tp, r_tp, s_ip, r_ip, s_fin, r_fin,
+    s_txt, r_txt, s_img, r_img, s_pair, r_pair, s_sib, r_sib, s_sibt, r_sibt, s_sibp, r_sibp,
+    s_row, r_row, s_col, r_col, s_loss, r_loss, s_tp, r_tp, s_ip, r_ip, s_fin, r_fin, s_load,
 ):
     x, yl, yh, z, c = where_am_i()
     q, k = z % 2, z // 2
@@ -62,10 +64,9 @@
     sibling = device(x, yl, yh, z, 1 - c)
 
     barrier = pltpu.get_barrier_semaphore()
-    partners = [to(in_column(dh, dk)) for dh, dk in COLUMN]
-    partners += [pair]
-    partners += [to(in_plane(dx, dy, dq)) for dq in range(2) for dx, dy in PLANE if dq or (dx, dy) != (0, 2)]
-    partners += [sibling]
+    partners = [to(in_column(0, dk)) for dk in FAR]
+    partners += [to(in_plane(dx, dy)) for dx, dy in PLANE]
+    partners += [pair, sibling]
     for partner in partners:
         pl.semaphore_signal(barrier, inc=1, device_id=partner, device_id_type=MESH)
 
@@ -76,9 +77,17 @@
     own_rows = image_rows(q, p)
     own_cols = pl.ds(pl.multiple_of(k * HALF, HALF), HALF)
     own_half = pl.ds(pl.multiple_of(yh * HALF, HALF), HALF)
-    img_all[feat, own_rows, :] = img_ref[...]
-    txt_all[feat, own_cols, :] = txt_ref[own_half, :]
+    own_block = img_all.at[feat, own_rows, :]
+    loads = [
+        pltpu.make_async_copy(img_hbm, own_block, s_load.at[0]),
+        pltpu.make_async_copy(txt_hbm, txt_own, s_load.at[1]),
+    ]
+    for load in loads:
+        load.start()
     col_own[...] = jnp.zeros_like(col_own)
+    for load in loads:
+        load.wait()
+    txt_all[feat, own_cols, :] = txt_own[own_half, :]
     pl.semaphore_wait(barrier, len(partners))
 
     started = []
@@ -91,19 +100,21 @@
         started.append(copy)
         return copy
 
-    txt_copies = []
-    for n, (dh, dk) in enumerate(COLUMN):
-        place = in_column(dh, dk)
-        half = pl.ds(pl.multiple_of(place[2] * HALF, HALF), HALF)
-        txt_copies.append(
-            send(txt_ref.at[half, :], txt_all.at[feat, own_cols, :], s_txt.at[n], r_txt.at[n], to(place))
-        )
-    own_block = img_all.at[feat, own_rows, :]
-    swap = send(img_ref, own_block, s_pair, r_pair, pair)
+    swap = send(own_block, own_block, s_pair, r_pair, pair)
+    other_half = pl.ds(pl.multiple_of((1 - yh) * HALF, HALF), HALF)
+    own_text = txt_all.at[feat, own_cols, :]
+    cross = send(txt_own.at[other_half, :], own_text, s_txt.at[1, 0], r_txt.at[1, 0], to(in_column(1, 0)))
+    txt_copies = {
+        (0, dk): send(own_text, own_text, s_txt.at[0, dk], r_txt.at[0, dk], to(in_column(0, dk))) for dk in FAR
+    }
     direct = [
-        send(img_ref, own_block, s_img.at[0, n], r_img.at[0, n], to(in_plane(dx, dy)))
+        send(own_block, own_block, s_img.at[0, n], r_img.at[0, n], to(in_plane(dx, dy)))
         for n, (dx, dy) in enumerate(PLANE)
     ]
+    cross.wait_recv()
+    cross_text = txt_all.at[2 * (1 - yh) + c, own_cols, :]
+    for dk in FAR:
+        txt_copies[1, dk] = send(cross_text, cross_text, s_txt.at[1, dk], r_txt.at[1, dk], to(in_column(0, dk)))
     swap.wait_recv()
     pair_block = img_all.at[feat, image_rows(1 - q, p), :]
     passed = [
@@ -111,25 +122,25 @@
         for n, (dx, dy) in enumerate(PLANE)
     ]
 
-    def share_image(slot, q0):
-        copies = []
-        for h in range(2):
-            part = img_all.at[2 * h + c, pl.ds(pl.multiple_of(q0 * 8 * ROWS, 8 * ROWS), 8 * ROWS), :]
-            copies.append(send(part, part, s_sib.at[slot, h], r_sib.at[slot, h], sibling))
-        return copies
-
     shared = []
     for copy in direct:
         copy.wait_recv()
-    shared += share_image(0, q)
-    for copy in txt_copies:
-        copy.wait_recv()
     for h in range(2):
-        part = txt_all.at[2 * h + c]
-        shared.append(send(part, part, s_sib.at[1, h], r_sib.at[1, h], sibling))
-    for copy in passed:
-        copy.wait_recv()
-    shared += share_image(2, 1 - q)
+        part = img_all.at[2 * h + c, pl.ds(pl.multiple_of(q * 8 * ROWS, 8 * ROWS), 8 * ROWS), :]
+        shared.append(send(part, part, s_sib.at[h], r_sib.at[h], sibling))
+    shared.append(send(pair_block, pair_block, s_sibp.at[0], r_sibp.at[0], sibling))
+    for dk in (0,) + FAR[::-1]:
+        for dh in range(2):
+            if dk:
+                txt_copies[dh, dk].wait_recv()
+            rows = pl.ds(pl.multiple_of(((k - dk + 8) % 8) * HALF, HALF), HALF)
+            part = txt_all.at[2 * ((yh + dh) % 2) + c, rows, :]
+            shared.append(send(part, part, s_sibt.at[dh, dk], r_sibt.at[dh, dk], sibling))
+    for n, (dx, dy) in enumerate(PLANE):
+        passed[n].wait_recv()
+        x2, yl2, yh2, _ = in_plane(-dx, -dy)
+        part = img_all.at[2 * yh2 + c, image_rows(1 - q, yl2 * NX + x2), :]
+        shared.append(send(part, part, s_sibp.at[n + 1], r_sibp.at[n + 1], sibling))
     for copy in shared:
         copy.wait_recv()
 
@@ -182,7 +193,7 @@
     col_own[pl.ds(1, 1), :] = lse[:, LANES:]
     col_slot = col_recv.at[k]
     col_copies = [
-        send(col_own, col_slot, s_col.at[dk], r_col.at[dk], to(in_column(0, dk))) for dk in (4, 3, 5, 2, 6, 1, 7)
+        send(col_own, col_slot, s_col.at[dk], r_col.at[dk], to(in_column(0, dk))) for dk in FAR
     ]
     col_slot[...] = col_own[...]
 
@@ -285,6 +296,7 @@
 
 def per_device(image_embeds, text_embeds, logit_scale):
     vmem = pl.BlockSpec(memory_space=pltpu.VMEM)
+    hbm = pl.BlockSpec(memory_space=pltpu.HBM)
     dma = pltpu.SemaphoreType.DMA
     column, plane = len(COLUMN), len(PLANE)
     loss, image_grad, text_grad = pl.pallas_call(
@@ -294,9 +306,10 @@
             jax.ShapeDtypeStruct((ROWS, FEATS), F32),
             jax.ShapeDtypeStruct((ROWS, FEATS), F32),
         ),
-        in_specs=[pl.BlockSpec(memory_space=pltpu.SMEM), vmem, vmem],
+        in_specs=[pl.BlockSpec(memory_space=pltpu.SMEM), hbm, hbm],
         out_specs=(vmem, vmem, vmem),
         scratch_shapes=[
+            pltpu.VMEM((ROWS, FEATS), BF16),
             pltpu.VMEM((4, IMG, FEATS), BF16),
             pltpu.VMEM((4, TXT, FEATS), BF16),
             pltpu.VMEM((IMG, TXT), F32),
@@ -317,16 +330,19 @@
             pltpu.VMEM((ROWS, LANES), F32),
             pltpu.VMEM((ROWS, FEATS), F32),
             pltpu.VMEM((ROWS, FEATS), F32),
-            dma((column,)), dma((column,)),
+            dma((2, 8)), dma((2, 8)),
             dma((2, plane)), dma((2, plane)),
             dma, dma,
-            dma((3, 2)), dma((3, 2)),
+            dma((2,)), dma((2,)),
+            dma((2, 8)), dma((2, 8)),
+            dma((16,)), dma((16,)),
             dma((2, 16)), dma((2, 16)),
             dma((8,)), dma((8,)),
             dma, dma,
             dma((column,)), dma((column,)),
             dma((2, plane)), dma((2, plane)),
             dma, dma,
+            dma((2,)),
         ],
         compiler_params=pltpu.CompilerParams(
             collective_id=0, has_side_effects=True, vmem_limit_bytes=48 << 20

time: 75.7 us -> 69.9 us (0.923)
  Pallas kernels: 71 us -> 64.7 us
    pallas_call x1, Pallas kernels: 71 us -> 64.7 us  [per_device(): pl.pallas_call(kernel, out_shape=(jax.ShapeDtypeStruct((1, ROWS), F32), j...]
where the time goes in v2:
time: 69.9 us; the launch traced here: 68.6 us
  Pallas kernels  64.7 us (93%)
  local copies, waits for them, and re-layouts  2.02 us (3%)
  between operations  1.3 us (2%)
    pallas_call x1, Pallas kernels, per_device(): pl.pallas_call(kernel, out_shape=(jax.ShapeDtypeStruct((1, ROWS), F32), j...  64.7 us
    unnamed x5, local copies, waits for them, and re-layouts  2.02 us

profile of v2, /device:TPU:1, one launch (start us, length us, event | category | flops | bytes accessed | tf_op | source)
XLA Modules:
  0.0 68.6 jit_solution(7543098379244638328)
XLA Ops:
  1.3 0.0 copy-start
  1.3 0.7 %copy-done = bf16[64,256]{1,0:T(8,128)(2,1)S(1)} copy-done((bf16[64,256]{1,0:T(8,128)(2,1)S(1)}, bf16[64,256]{1,0:T(8,128)(2,1)}, u32[]{:S(2)}) %copy-start) | copy-done | bytes 32792
  2.0 0.0 copy-start.1
  2.0 0.8 %copy-done.1 = bf16[64,256]{1,0:T(8,128)(2,1)S(1)} copy-done((bf16[64,256]{1,0:T(8,128)(2,1)S(1)}, bf16[64,256]{1,0:T(8,128)(2,1)}, u32[]{:S(2)}) %copy-start.1) | copy-done | bytes 32792
  2.8 64.7 %shard_map.58 = (f32[1,64]{1,0:T(1,128)S(1)}, f32[64,256]{1,0:T(8,128)S(1)}, f32[64,256]{1,0:T(8,128)S(1)}) custom-call(f32[1]{0:T(128)} %copy.7.scale_ref, bf16[64,256]{1,0:T(8,128)(2,1)S(1)} %copy-done, bf16[64,256]{1,0:T(8,128)(2,1)S(1)} %copy-done.1), custom_call_target="tpu_custom_call" | custom-call | tf_op jit(solution)/shard_map/pallas_call | solution.py:302
  67.5 0.7 broadcast_multiply_fusion
  68.1 0.5 copy.8
Async XLA Ops:
  1.3 0.8 %copy-start = (bf16[64,256]{1,0:T(8,128)(2,1)S(1)}, bf16[64,256]{1,0:T(8,128)(2,1)}, u32[]{:S(2)}) copy-start(bf16[64,256]{1,0:T(8,128)(2,1)} %img_hbm.1) | copy-start | bytes 98308
  2.0 0.8 %copy-start.1 = (bf16[64,256]{1,0:T(8,128)(2,1)S(1)}, bf16[64,256]{1,0:T(8,128)(2,1)}, u32[]{:S(2)}) copy-start(bf16[64,256]{1,0:T(8,128)(2,1)} %txt_hbm.1) | copy-start | bytes 98308

commit v3 on v2

--- a/solution.py
+++ b/solution.py
@@ -18,7 +18,7 @@
 TXT = 8 * HALF
 LANES = 128
 
-PLANE = [(dx, dy) for dx in range(NX) for dy in range(NY) if dx or dy]
+PLANE = sorted([(dx, dy) for dx in range(NX) for dy in range(NY) if dx or dy], key=lambda o: min(o[0], 4 - o[0]) + min(o[1], 4 - o[1]))
 FAR = (4, 3, 5, 2, 6, 1, 7)
 COLUMN = [(dh, dk) for dk in FAR for dh in range(2)] + [(1, 0)]
 
@@ -111,10 +111,6 @@
         send(own_block, own_block, s_img.at[0, n], r_img.at[0, n], to(in_plane(dx, dy)))
         for n, (dx, dy) in enumerate(PLANE)
     ]
-    cross.wait_recv()
-    cross_text = txt_all.at[2 * (1 - yh) + c, own_cols, :]
-    for dk in FAR:
-        txt_copies[1, dk] = send(cross_text, cross_text, s_txt.at[1, dk], r_txt.at[1, dk], to(in_column(0, dk)))
     swap.wait_recv()
     pair_block = img_all.at[feat, image_rows(1 - q, p), :]
     passed = [
@@ -122,6 +118,10 @@
         for n, (dx, dy) in enumerate(PLANE)
     ]
 
+    cross.wait_recv()
+    cross_text = txt_all.at[2 * (1 - yh) + c, own_cols, :]
+    for dk in FAR:
+        txt_copies[1, dk] = send(cross_text, cross_text, s_txt.at[1, dk], r_txt.at[1, dk], to(in_column(0, dk)))
     shared = []
     for copy in direct:
         copy.wait_recv()
@@ -163,24 +163,8 @@
             total = term if total is None else total + term
         value = factor * total
         logits[rows, :] = value
-        largest = jnp.max(value, axis=1, keepdims=True)
-        shifted = jnp.exp(value - largest)
-        e_row[rows, :] = shifted
-        lse = largest + jnp.log(jnp.sum(shifted, axis=1, keepdims=True))
-        row_own[pl.ds(b, 1), :] = to_lanes(lse)
-        row_max[pl.ds(b, 1), :] = to_lanes(largest)
         block_max = jnp.max(value, axis=0, keepdims=True)
         col_max = block_max if col_max is None else jnp.maximum(col_max, block_max)
-
-    row_slot = row_recv.at[q * 16 + (yh * 2 + yl) * NX + x]
-    row_copies = []
-    for dq in range(2):
-        for n, (dx, dy) in enumerate([(0, 0)] + PLANE):
-            if dq or n:
-                row_copies.append(
-                    send(row_own, row_slot, s_row.at[dq, n], r_row.at[dq, n], to(in_plane(dx, dy, dq)))
-                )
-    row_slot[...] = row_own[...]
 
     col_sum = jnp.zeros((1, TXT), F32)
     for b in range(IMG // LANES):
@@ -196,6 +180,26 @@
         send(col_own, col_slot, s_col.at[dk], r_col.at[dk], to(in_column(0, dk))) for dk in FAR
     ]
     col_slot[...] = col_own[...]
+
+    for b in range(IMG // LANES):
+        rows = pl.ds(b * LANES, LANES)
+        value = logits[rows, :]
+        largest = jnp.max(value, axis=1, keepdims=True)
+        shifted = jnp.exp(value - largest)
+        e_row[rows, :] = shifted
+        lse = largest + jnp.log(jnp.sum(shifted, axis=1, keepdims=True))
+        row_own[pl.ds(b, 1), :] = to_lanes(lse)
+        row_max[pl.ds(b, 1), :] = to_lanes(largest)
+
+    row_slot = row_recv.at[q * 16 + (yh * 2 + yl) * NX + x]
+    row_copies = []
+    for dq in range(2):
+        for n, (dx, dy) in enumerate([(0, 0)] + PLANE):
+            if dq or n:
+                row_copies.append(
+                    send(row_own, row_slot, s_row.at[dq, n], r_row.at[dq, n], to(in_plane(dx, dy, dq)))
+                )
+    row_slot[...] = row_own[...]
 
     for copy in row_copies:
         copy.wait_recv()
@@ -238,19 +242,6 @@
     loss_part = loss_all.at[own_half, :]
     loss_copy = send(loss_part, loss_part, s_loss, r_loss, to(in_column(1, 0)))
 
-    for h in range(2):
-        t_part[h] = lax.dot_general(
-            grad[...], img_all[2 * h + c], (((0,), (0,)), ((), ())), preferred_element_type=F32
-        ).astype(BF16)
-    tp_copies = []
-    for n, (dh, dk) in enumerate(COLUMN):
-        place = in_column(dh, dk)
-        rows = pl.ds(pl.multiple_of(((k + dk) % 8) * HALF, HALF), HALF)
-        tp_copies.append(
-            send(t_part.at[place[2], rows, :], t_recv.at[yh, k], s_tp.at[n], r_tp.at[n], to(place))
-        )
-    t_recv[yh, k] = t_part[yh, own_cols, :]
-
     ip_copies = []
     for turn in range(2):
         q2 = 1 - q if turn == 0 else q
@@ -267,6 +258,19 @@
             copies.append(send(block, i_recv.at[turn, slot], s_ip.at[turn, n], r_ip.at[turn, n], to(place)))
         i_recv[turn, slot] = i_part[yh, image_rows(q2, p), :]
         ip_copies.append(copies)
+
+    for h in range(2):
+        t_part[h] = lax.dot_general(
+            grad[...], img_all[2 * h + c], (((0,), (0,)), ((), ())), preferred_element_type=F32
+        ).astype(BF16)
+    tp_copies = []
+    for n, (dh, dk) in enumerate(COLUMN):
+        place = in_column(dh, dk)
+        rows = pl.ds(pl.multiple_of(((k + dk) % 8) * HALF, HALF), HALF)
+        tp_copies.append(
+            send(t_part.at[place[2], rows, :], t_recv.at[yh, k], s_tp.at[n], r_tp.at[n], to(place))
+        )
+    t_recv[yh, k] = t_part[yh, own_cols, :]
 
     def total_of(ref, count):
         value = ref[0].astype(F32)

time: 69.9 us -> 67.4 us (0.964); the launches traced: 68.6 us -> 67.2 us
  Pallas kernels: 64.7 us -> 63.2 us
    pallas_call x1, Pallas kernels: 64.7 us -> 63.2 us  [per_device(): pl.pallas_call(kernel, out_shape=(jax.ShapeDtypeStruct((1, ROWS), F32), j...]
where the time goes in v3:
time: 67.4 us; the launch traced here: 67.2 us
  Pallas kernels  63.2 us (94%)
  local copies, waits for them, and re-layouts  2.02 us (3%)
  between operations  1.3 us (2%)
    pallas_call x1, Pallas kernels, per_device(): pl.pallas_call(kernel, out_shape=(jax.ShapeDtypeStruct((1, ROWS), F32), j...  63.2 us
    unnamed x5, local copies, waits for them, and re-layouts  2.02 us

profile of v3, /device:TPU:1, one launch (start us, length us, event | category | flops | bytes accessed | tf_op | source)
XLA Modules:
  0.0 67.2 jit_solution(214951408875792287)
XLA Ops:
  1.3 0.0 copy-start
  1.3 0.7 %copy-done = bf16[64,256]{1,0:T(8,128)(2,1)S(1)} copy-done((bf16[64,256]{1,0:T(8,128)(2,1)S(1)}, bf16[64,256]{1,0:T(8,128)(2,1)}, u32[]{:S(2)}) %copy-start) | copy-done | bytes 32792
  2.0 0.0 copy-start.1
  2.0 0.8 %copy-done.1 = bf16[64,256]{1,0:T(8,128)(2,1)S(1)} copy-done((bf16[64,256]{1,0:T(8,128)(2,1)S(1)}, bf16[64,256]{1,0:T(8,128)(2,1)}, u32[]{:S(2)}) %copy-start.1) | copy-done | bytes 32792
  2.8 63.2 %shard_map.58 = (f32[1,64]{1,0:T(1,128)S(1)}, f32[64,256]{1,0:T(8,128)S(1)}, f32[64,256]{1,0:T(8,128)S(1)}) custom-call(f32[1]{0:T(128)} %copy.7.scale_ref, bf16[64,256]{1,0:T(8,128)(2,1)S(1)} %copy-done, bf16[64,256]{1,0:T(8,128)(2,1)S(1)} %copy-done.1), custom_call_target="tpu_custom_call" | custom-call | tf_op jit(solution)/shard_map/pallas_call | solution.py:306
  66.0 0.7 broadcast_multiply_fusion
  66.6 0.5 copy.8
Async XLA Ops:
  1.3 0.8 %copy-start = (bf16[64,256]{1,0:T(8,128)(2,1)S(1)}, bf16[64,256]{1,0:T(8,128)(2,1)}, u32[]{:S(2)}) copy-start(bf16[64,256]{1,0:T(8,128)(2,1)} %img_hbm.1) | copy-start | bytes 98308
  2.0 0.8 %copy-start.1 = (bf16[64,256]{1,0:T(8,128)(2,1)S(1)}, bf16[64,256]{1,0:T(8,128)(2,1)}, u32[]{:S(2)}) copy-start(bf16[64,256]{1,0:T(8,128)(2,1)} %txt_hbm.1) | copy-start | bytes 98308

commit v4 on v3

--- a/solution.py
+++ b/solution.py
@@ -303,6 +303,7 @@
     hbm = pl.BlockSpec(memory_space=pltpu.HBM)
     dma = pltpu.SemaphoreType.DMA
     column, plane = len(COLUMN), len(PLANE)
+    in_hbm = functools.partial(pltpu.with_memory_space_constraint, memory_space=pltpu.HBM)
     loss, image_grad, text_grad = pl.pallas_call(
         kernel,
         out_shape=(
@@ -351,7 +352,7 @@
         compiler_params=pltpu.CompilerParams(
             collective_id=0, has_side_effects=True, vmem_limit_bytes=48 << 20
         ),
-    )(logit_scale, image_embeds, text_embeds)
+    )(logit_scale, in_hbm(image_embeds), in_hbm(text_embeds))
     factor = logit_scale[0]
     return loss.reshape(ROWS), factor * image_grad, factor * text_grad
 

time: 67.4 us -> 65.8 us (0.976)
  local copies, waits for them, and re-layouts: 2.02 us -> 0.51 us
    unnamed x5 -> x1, local copies, waits for them, and re-layouts: 2.02 us -> 0.51 us
where the time goes in v4:
time: 65.8 us; the launch traced here: 65.6 us
  Pallas kernels  63.2 us (96%)
  between operations  1.29 us (2%)
  other arithmetic  0.66 us (1%)
    pallas_call x1, Pallas kernels, per_device(): pl.pallas_call(kernel, out_shape=(jax.ShapeDtypeStruct((1, ROWS), F32), j...  63.2 us

profile of v4, /device:TPU:1, one launch (start us, length us, event | category | flops | bytes accessed | tf_op | source)
XLA Modules:
  0.0 65.6 jit_solution(9472742949928366856)
XLA Ops:
  1.3 63.2 %shard_map.58 = (f32[1,64]{1,0:T(1,128)S(1)}, f32[64,256]{1,0:T(8,128)S(1)}, f32[64,256]{1,0:T(8,128)S(1)}) custom-call(f32[1]{0:T(128)} %copy.7.scale_ref, bf16[64,256]{1,0:T(8,128)(2,1)} %img_hbm.1, bf16[64,256]{1,0:T(8,128)(2,1)} %txt_hbm.1), custom_call_target="tpu_custom_call" | custom-call | tf_op jit(solution)/shard_map/pallas_call | solution.py:307
  64.5 0.7 %broadcast_multiply_fusion = (f32[64,256]{1,0:T(8,128)}, f32[64,256]{1,0:T(8,128)}) fusion(f32[64,256]{1,0:T(8,128)S(1)} %get-tuple-element.8, f32[]{:T(128)} %bitcast.2, f32[64,256]{1,0:T(8,128)S(1)} %get-tuple-element.7), kind=kLoop, calls=%fused_computation | loop fusion | flops 32768 | bytes 262148 | tf_op jit(solution)/shard_map/mul | solution.py:357
  65.1 0.5 copy.8

commit v5 on v4

--- a/solution.py
+++ b/solution.py
@@ -217,10 +217,32 @@
     col_lse = jnp.concatenate([col_total[0:1], col_total[1:2]], axis=1)
     col_mul = 0.5 * jnp.exp(col_max - col_lse)
 
-    for b in range(IMG // LANES):
-        rows = pl.ds(b * LANES, LANES)
-        row_factor = to_rows(row_mul[pl.ds(b, 1), :])
-        grad[rows, :] = (e_row[rows, :] * row_factor + e_col[rows, :] * col_mul).astype(BF16)
+    def gradient(q2):
+        for b in range(4):
+            rows = pl.ds(pl.multiple_of(q2 * (8 * ROWS) + b * LANES, LANES), LANES)
+            row_factor = to_rows(row_mul[pl.ds(q2 * 4 + b, 1), :])
+            grad[rows, :] = (e_row[rows, :] * row_factor + e_col[rows, :] * col_mul).astype(BF16)
+
+    ip_copies = []
+    def image_turn(turn):
+        q2 = 1 - q if turn == 0 else q
+        rows = pl.ds(pl.multiple_of(q2 * 8 * ROWS, 8 * ROWS), 8 * ROWS)
+        for h in range(2):
+            i_part[h, rows, :] = jnp.dot(
+                grad[rows, :], txt_all[2 * h + c], preferred_element_type=F32
+            ).astype(BF16)
+        slot = (yh * 2 + yl) * NX + x
+        copies = []
+        for n, (dx, dy) in enumerate(PLANE):
+            place = in_plane(dx, dy)
+            block = i_part.at[place[2], image_rows(q2, place[1] * NX + place[0]), :]
+            copies.append(send(block, i_recv.at[turn, slot], s_ip.at[turn, n], r_ip.at[turn, n], to(place)))
+        i_recv[turn, slot] = i_part[yh, image_rows(q2, p), :]
+        ip_copies.append(copies)
+
+    gradient(1 - q)
+    image_turn(0)
+    gradient(q)
     first = (q * 8 + p) * ROWS + yh * HALF
     diag_rows = pl.ds(pl.multiple_of(first, HALF), HALF)
     row_id = lax.broadcasted_iota(jnp.int32, (HALF, LANES), 0)
@@ -235,29 +257,13 @@
     grad[diag_rows, :] = (
         e_row[diag_rows, :] * diag_mul + e_col[diag_rows, :] * col_mul - unit.astype(F32)
     ).astype(BF16)
+    image_turn(1)
     loss = jnp.sum(
         jnp.where(unit, 0.5 * (diag_lse + col_lse) - logits[diag_rows, :], 0.0), axis=1, keepdims=True
     )
     loss_all[own_half, :] = jnp.broadcast_to(loss, (HALF, LANES))
     loss_part = loss_all.at[own_half, :]
     loss_copy = send(loss_part, loss_part, s_loss, r_loss, to(in_column(1, 0)))
-
-    ip_copies = []
-    for turn in range(2):
-        q2 = 1 - q if turn == 0 else q
-        rows = pl.ds(pl.multiple_of(q2 * 8 * ROWS, 8 * ROWS), 8 * ROWS)
-        for h in range(2):
-            i_part[h, rows, :] = jnp.dot(
-                grad[rows, :], txt_all[2 * h + c], preferred_element_type=F32
-            ).astype(BF16)
-        slot = (yh * 2 + yl) * NX + x
-        copies = []
-        for n, (dx, dy) in enumerate(PLANE):
-            place = in_plane(dx, dy)
-            block = i_part.at[place[2], image_rows(q2, place[1] * NX + place[0]), :]
-            copies.append(send(block, i_recv.at[turn, slot], s_ip.at[turn, n], r_ip.at[turn, n], to(place)))
-        i_recv[turn, slot] = i_part[yh, image_rows(q2, p), :]
-        ip_copies.append(copies)
 
     for h in range(2):
         t_part[h] = lax.dot_general(

time: 65.8 us -> 65.8 us (level)
  no operation moved by 1% of the time
where the time goes in v5:
time: 65.8 us; the launch traced here: 65.6 us
  Pallas kernels  63.2 us (96%)
  between operations  1.29 us (2%)
  other arithmetic  0.66 us (1%)
    pallas_call x1, Pallas kernels, per_device(): pl.pallas_call(kernel, out_shape=(jax.ShapeDtypeStruct((1, ROWS), F32), j...  63.2 us

profile of v5, /device:TPU:1, one launch (start us, length us, event | category | flops | bytes accessed | tf_op | source)
XLA Modules:
  0.0 65.6 jit_solution(3359480597639018028)
XLA Ops:
  1.3 63.2 %shard_map.58 = (f32[1,64]{1,0:T(1,128)S(1)}, f32[64,256]{1,0:T(8,128)S(1)}, f32[64,256]{1,0:T(8,128)S(1)}) custom-call(f32[1]{0:T(128)} %copy.7.scale_ref, bf16[64,256]{1,0:T(8,128)(2,1)} %img_hbm.1, bf16[64,256]{1,0:T(8,128)(2,1)} %txt_hbm.1), custom_call_target="tpu_custom_call" | custom-call | tf_op jit(solution)/shard_map/pallas_call | solution.py:313
  64.4 0.7 %broadcast_multiply_fusion = (f32[64,256]{1,0:T(8,128)}, f32[64,256]{1,0:T(8,128)}) fusion(f32[64,256]{1,0:T(8,128)S(1)} %get-tuple-element.8, f32[]{:T(128)} %bitcast.2, f32[64,256]{1,0:T(8,128)S(1)} %get-tuple-element.7), kind=kLoop, calls=%fused_computation | loop fusion | flops 32768 | bytes 262148 | tf_op jit(solution)/shard_map/mul | solution.py:363
  65.1 0.5 copy.8
